TPU v7x, 128 devices: a whole 4x4x4 slice. The times are simulated.
128 devices in a mesh: gx: 32 (over y, x, core), gy: 4 (over z).
Axes of the slice: x: 4, y: 4, z: 4, core: 2. Of those that a mesh axis runs over, the one named last changes fastest.
Arguments:
- velocity: bfloat16 [3, 4, 4096, 2048], P(None, None, 'gx', 'gy'), may hold values from -24 to 24
- block_ids: int32 [32, 4, 128, 4], P('gx', 'gy'), may hold values from 0 to 1023
- counts: int32 [32, 4, 128], P('gx', 'gy'), may hold values from 0 to 4, as said below
- positions: float32 [3, 32, 4, 128, 128], P(None, 'gx', 'gy'), may hold values from 0 to 1
Outputs:
- filtered: bfloat16 [2, 3, 4, 4096, 2048], P(None, None, None, 'gx', 'gy')
- sampled: float32 [2, 3, 32, 4, 128, 128], P(None, None, 'gx', 'gy')
Inputs may be any that keep to these rules, and one draw needn't show every extreme that they name: `block_ids`: a listed block number of the sending device. `counts`: used slots from a device to an owner; some owners get 4 from every device.
All inputs are finite; a program needn't handle non-finite values.
Results may differ from a plain program's by a relative error of at most 0.006.
Values may be sent and summed in bfloat16 or wider, within the bound.
A program may use at most 128 MiB of HBM per device.

v0:
```python
import jax
import jax.numpy as jnp
import ml_dtypes
import numpy as np
from jax import lax
from jax.experimental import pallas as pl
from jax.experimental.pallas import tpu as pltpu
from jax.sharding import PartitionSpec as P

GX, GY = 32, 4
DEVICES = GX * GY
PLANES = 12
ROWS, COLS = 128, 512
REACH = 8
CAP = 4
SIGMAS = (1.5, 3.0)
GROUP = 4
MESH = pl.DeviceIdType.MESH
BF16, F32 = jnp.bfloat16, jnp.float32


def make_taps():
    offsets = np.arange(2 * REACH + 1, dtype=np.float32) - np.float32(REACH)
    stacked = []
    for deviation in SIGMAS:
        profile = np.exp(-offsets * offsets / np.float32(2.0 * deviation * deviation))
        stacked.append(profile / np.sum(profile))
    return np.stack(stacked).astype(ml_dtypes.bfloat16).astype(np.float32)


def tap_lookup(taps, index):
    inside = (index >= 0) & (index <= 2 * REACH)
    return np.where(inside, taps[:, np.clip(index, 0, 2 * REACH)], 0.0)


def constant_tables():
    taps = make_taps()
    own = np.arange(ROWS)
    r = np.arange(16)
    tables = []
    for variant in range(3):
        if variant < 2:
            valid = (r // 8) == variant
            before, after = r % 8 - 8, ROWS + r % 8
        else:
            valid = np.ones(16, bool)
            before, after = r - 16, ROWS + r
        where_k = np.concatenate([own, before, after])
        keep = np.concatenate([np.ones(ROWS, bool), valid, valid])
        index = where_k[None, :] - own[:, None] + REACH
        tables.append((tap_lookup(taps, index) * keep).reshape(2 * ROWS, -1))
    along_x = np.stack(tables)
    k, n = np.arange(512)[:, None], np.arange(256)[None, :]
    along_y = tap_lookup(taps, k - 128 - n + REACH)
    plane, lane = np.arange(PLANES * 128)[:, None] // 128, np.arange(PLANES * 128)[:, None] % 128
    n = np.arange(128)[None, :]
    last = (lane >= 120) & (n == 8 * plane + lane - 120)
    first = (lane < 8) & (n == 8 * plane + lane)
    pack = np.stack([first, last]).astype(np.float32)
    unpack = np.concatenate([last.T, first.T], axis=0).astype(np.float32)
    return [np.asarray(t, np.float32).astype(ml_dtypes.bfloat16) for t in (along_x, along_y, pack, unpack)]


def hat(distance):
    return jnp.maximum(0.0, 1.0 - jnp.abs(distance))


def kernel(
    vel_hbm, ids, used, pos_hbm, bx_hbm, by_hbm, pack_hbm, unpack_hbm,
    filt_hbm, samp_ref,
    vel, pos, bx, by, pack, unpack,
    rows_first, rows_last, rows_after, rows_before,
    cols_first, cols_last, cols_after, cols_before, corners,
    halo, filt, table,
    pos_send, pos_recv, out_send, out_recv,
    in_sems, halo_send, halo_recv, pos_sems, out_sems, filt_sem,
):
    ix, iy = lax.axis_index("gx"), lax.axis_index("gy")
    me = ix * GY + iy

    loads = [
        pltpu.make_async_copy(src, dst, in_sems.at[i])
        for i, (src, dst) in enumerate(
            ((pos_hbm, pos), (vel_hbm, vel), (pack_hbm, pack), (unpack_hbm, unpack), (bx_hbm, bx), (by_hbm, by))
        )
    ]
    for load in loads:
        load.start()

    barrier = pltpu.get_barrier_semaphore()

    def device_of(number):
        return (lax.shift_right_logical(number, 2), number & (GY - 1))

    @pl.loop(1, DEVICES)
    def _(k):
        pl.semaphore_signal(barrier, 1, device_id=device_of((me + k) & (DEVICES - 1)), device_id_type=MESH)

    loads[0].wait()
    for c in range(3):
        pos_send[:, c, :] = pos[c]
    pos_send[:, 3, :] = pos[0]
    pos_recv[me] = pos_send[me]

    for load in loads[1:3]:
        load.wait()
    for pair in range(PLANES // 2):
        for buf, start, part in ((rows_first, 0, 0), (rows_last, ROWS - 16, 8)):
            low = vel[2 * pair, start : start + 16, :].astype(F32)[part : part + 8]
            high = vel[2 * pair + 1, start : start + 16, :].astype(F32)[part : part + 8]
            buf[pair] = jnp.concatenate([low, high], axis=0).astype(BF16)
    for buf, side, start in ((cols_first, 0, 0), (cols_last, 1, COLS - 128)):
        edge = jnp.concatenate([vel[p, :, start : start + 128] for p in range(PLANES)], axis=1)
        buf[...] = jnp.dot(edge, pack[side], preferred_element_type=F32).astype(BF16)

    pl.semaphore_wait(barrier, DEVICES - 1)

    x_next, x_prev = (ix + 1) & (GX - 1), (ix + GX - 1) & (GX - 1)
    y_next, y_prev = (iy + 1) & (GY - 1), (iy + GY - 1) & (GY - 1)
    top, bottom = pl.ds(0, 16), pl.ds(ROWS - 16, 16)
    halo_copies = [
        pltpu.make_async_remote_copy(
            src, dst, halo_send.at[i], halo_recv.at[i], device_id=target, device_id_type=MESH
        )
        for i, (src, dst, target) in enumerate(
            (
                (rows_first, rows_after, (x_prev, iy)),
                (rows_last, rows_before, (x_next, iy)),
                (cols_first, cols_after, (ix, y_prev)),
                (cols_last, cols_before, (ix, y_next)),
                (cols_last.at[bottom], corners.at[0], (x_next, y_next)),
                (cols_last.at[top], corners.at[1], (x_prev, y_next)),
                (cols_first.at[bottom], corners.at[2], (x_next, y_prev)),
                (cols_first.at[top], corners.at[3], (x_prev, y_prev)),
            )
        )
    ]
    for copy in halo_copies:
        copy.start()

    @pl.loop(1, DEVICES)
    def _(k):
        other = (me + k) & (DEVICES - 1)
        pltpu.make_async_remote_copy(
            pos_send.at[other], pos_recv.at[me], pos_sems.at[0], pos_sems.at[1],
            device_id=device_of(other), device_id_type=MESH,
        ).start()

    for load in loads[3:]:
        load.wait()
    for copy in halo_copies:
        copy.wait_recv()

    packed = jnp.concatenate(
        [
            jnp.concatenate([cols_before[...], corners[0], corners[1]], axis=0),
            jnp.concatenate([cols_after[...], corners[2], corners[3]], axis=0),
        ],
        axis=1,
    )
    for p in range(PLANES):
        lanes = pl.ds(128 * p, 128)
        spread = jnp.dot(packed, unpack[:, lanes], preferred_element_type=F32).astype(BF16)
        halo[p] = jnp.dot(bx[2], spread, preferred_element_type=F32).astype(BF16)

    @pl.loop(0, PLANES // 2)
    def _(pair):
        smooth = []
        for parity in range(2):
            tall = jnp.concatenate([vel[2 * pair + parity], rows_before[pair], rows_after[pair]], axis=0)
            smooth.append(jnp.dot(bx[parity], tall, preferred_element_type=F32).astype(BF16))
        for width in range(2):
            part = slice(width * ROWS, (width + 1) * ROWS)
            for half in range(2):
                results = []
                for parity in range(2):
                    edge = halo[2 * pair + parity, part, :]
                    inner = smooth[parity][part]
                    wide = (
                        jnp.concatenate([edge, inner[:, :384]], axis=1)
                        if half == 0
                        else jnp.concatenate([inner[:, 128:], edge], axis=1)
                    )
                    got = jnp.dot(wide, by[width], preferred_element_type=F32)
                    filt[width * PLANES + 2 * pair + parity, :, 256 * half : 256 * half + 256] = got.astype(BF16)
                    results.append(got)
                first_row = pl.multiple_of(width * PLANES * 8 + pair * 16, 16)
                for block_row in range(ROWS // 8):
                    both = jnp.concatenate(
                        [got[8 * block_row : 8 * block_row + 8] for got in results], axis=0
                    ).astype(BF16)
                    for tile in range(2):
                        table[block_row * 4 + half * 2 + tile, pl.ds(first_row, 16), :] = both[
                            :, 128 * tile : 128 * tile + 128
                        ]

    store = pltpu.make_async_copy(filt, filt_hbm, filt_sem)
    store.start()

    others = pl.ds(0, DEVICES - 1)
    pltpu.make_async_remote_copy(
        pos_send.at[others], pos_recv.at[others], pos_sems.at[0], pos_sems.at[1],
        device_id=(x_next, iy), device_id_type=MESH,
    ).wait()

    lane_slot = lax.shift_right_logical(lax.broadcasted_iota(jnp.int32, (1, 128), 1), 5)
    rows128 = lax.broadcasted_iota(jnp.int32, (128, 128), 0).astype(F32)
    rows8 = lax.broadcasted_iota(jnp.int32, (8, 128), 0).astype(F32)

    def sample(owner):
        numbers = [ids[q, owner] for q in range(CAP)]
        blocks = jnp.concatenate([table[lax.shift_right_logical(n, 4)] for n in numbers], axis=1)
        place = [(n & 15) * 8 for n in numbers]
        offset = jnp.where(
            lane_slot < 2,
            jnp.where(lane_slot == 0, place[0], place[1]),
            jnp.where(lane_slot == 2, place[2], place[3]),
        ).astype(F32)
        spot = pos_recv[owner]
        along_x, along_y, along_z = 7.0 * spot[0:1], 7.0 * spot[1:2], 3.0 * spot[2:3]
        target = jnp.where(lane_slot < used[0, owner], offset + along_y, -1000.0)
        weights = jnp.concatenate(
            [hat(rows128 - jnp.where(lane_slot == q, target, -1000.0)).astype(BF16) for q in range(CAP)], axis=0
        )
        picked = jnp.dot(blocks, weights, preferred_element_type=F32).reshape(6, 4, 8, 128)
        weight_x = hat(rows8 - along_x)
        total = picked[:, 0] * (weight_x * hat(along_z))
        for z in range(1, 4):
            total = total + picked[:, z] * (weight_x * hat(along_z - float(z)))
        out_send[owner] = jnp.sum(total, axis=1)

    def reply(owner):
        pltpu.make_async_remote_copy(
            out_send.at[owner], out_recv.at[me], out_sems.at[0], out_sems.at[1],
            device_id=device_of(owner), device_id_type=MESH,
        ).start()

    first = [(me + k) & (DEVICES - 1) for k in range(GROUP)]
    for owner in first:
        sample(owner)
    for owner in first[1:]:
        reply(owner)
    out_recv[me] = out_send[me]

    @pl.loop(1, DEVICES // GROUP)
    def _(group):
        owners = [(me + group * GROUP + k) & (DEVICES - 1) for k in range(GROUP)]
        for owner in owners:
            sample(owner)
        for owner in owners:
            reply(owner)

    store.wait()
    for copy in halo_copies:
        copy.wait_send()
    pltpu.make_async_remote_copy(
        out_send.at[others], out_recv.at[others], out_sems.at[0], out_sems.at[1],
        device_id=(x_next, iy), device_id_type=MESH,
    ).wait()
    for c in range(6):
        samp_ref[c] = out_recv[:, c, :]


def body(velocity, block_ids, counts, positions):
    tables = [jnp.asarray(t) for t in constant_tables()]
    hbm = pl.BlockSpec(memory_space=pl.ANY)
    smem = pl.BlockSpec(memory_space=pltpu.SMEM)
    vmem = pl.BlockSpec(memory_space=pltpu.VMEM)
    filtered, sampled = pl.pallas_call(
        kernel,
        out_shape=(
            jax.ShapeDtypeStruct((2 * PLANES, ROWS, COLS), BF16),
            jax.ShapeDtypeStruct((6, DEVICES, 128), F32),
        ),
        in_specs=[hbm, smem, smem, hbm, hbm, hbm, hbm, hbm],
        out_specs=(hbm, vmem),
        scratch_shapes=[
            pltpu.VMEM((PLANES, ROWS, COLS), BF16),
            pltpu.VMEM((3, DEVICES, 128), F32),
            *[pltpu.VMEM(t.shape, BF16) for t in tables],
            *[pltpu.VMEM((PLANES // 2, 16, COLS), BF16)] * 4,
            *[pltpu.VMEM((ROWS, 128), BF16)] * 4,
            pltpu.VMEM((4, 16, 128), BF16),
            pltpu.VMEM((PLANES, 2 * ROWS, 128), BF16),
            pltpu.VMEM((2 * PLANES, ROWS, COLS), BF16),
            pltpu.VMEM((64, 192, 128), BF16),
            pltpu.VMEM((DEVICES, 4, 128), F32),
            pltpu.VMEM((DEVICES, 4, 128), F32),
            pltpu.VMEM((DEVICES, 6, 128), F32),
            pltpu.VMEM((DEVICES, 6, 128), F32),
            pltpu.SemaphoreType.DMA((6,)),
            pltpu.SemaphoreType.DMA((8,)),
            pltpu.SemaphoreType.DMA((8,)),
            pltpu.SemaphoreType.DMA((2,)),
            pltpu.SemaphoreType.DMA((2,)),
            pltpu.SemaphoreType.DMA,
        ],
        compiler_params=pltpu.CompilerParams(
            collective_id=0, has_side_effects=True, vmem_limit_bytes=63 * 1024 * 1024
        ),
        name="filter_and_sample",
    )(
        velocity.reshape(PLANES, ROWS, COLS),
        block_ids.reshape(DEVICES, CAP).T,
        counts.reshape(1, DEVICES),
        positions.reshape(3, DEVICES, 128),
        *tables,
    )
    return filtered.reshape(2, 3, 4, ROWS, COLS), sampled.reshape(2, 3, 1, 1, DEVICES, 128)


def solution(mesh):
    return jax.shard_map(
        body,
        mesh=mesh,
        in_specs=(
            P(None, None, "gx", "gy"),
            P("gx", "gy", None, None),
            P("gx", "gy", None),
            P(None, "gx", "gy", None, None),
        ),
        out_specs=(P(None, None, None, "gx", "gy"), P(None, None, "gx", "gy", None, None)),
        check_vma=False,
    )
```

profile of v0, /device:TPU:0, one launch (start us, length us, event | category | flops | bytes accessed | tf_op | source)
XLA Modules:
  0.0 46.0 jit_solution(11084802302698782639)
XLA Ops:
  0.6 40.7 %filter_and_sample.1 = (bf16[24,128,512]{2,1,0:T(8,128)(2,1)}, f32[6,128,128]{2,1,0:T(8,128)}) custom-call(bf16[12,128,512]{2,1,0:T(8,128)(2,1)} %bitcast.11, s32[4,128]{1,0:T(4,128)} %bitcast.14, s32[1,128]{1,0:T(1,128)} %bitcast.15, f32[3,128,128]{2,1,0:T(8,128)} %bitcast.13, bf16[3,256,160]{2,1,0:T(8,128)(2,1)} %constant.8.clone.bx_hbm, ...), custom_call_target="tpu_custom_call" | custom-call | tf_op jit(solution)/shard_map/filter_and_sample/pallas_call | solution.py:269
  41.3 0.0 copy-start
  41.4 3.9 %copy.13 = bf16[2,3,4,128,512]{4,3,2,1,0:T(8,128)(2,1)} copy(bf16[2,3,4,128,512]{4,3,2,1,0:T(8,128)(2,1)} %bitcast.10) | data formatting | bytes 6291456
  45.3 0.0 copy-done
  45.3 0.7 %copy.14 = f32[2,3,1,1,128,128]{5,4,3,2,1,0:T(8,128)} copy(f32[2,3,1,1,128,128]{5,4,3,2,1,0:T(8,128)S(1)} %bitcast.12) | data formatting | bytes 786432
Async XLA Ops:
  41.3 3.9 %copy-start = (f32[6,128,128]{2,1,0:T(8,128)S(1)}, f32[6,128,128]{2,1,0:T(8,128)}, u32[]{:S(2)}) copy-start(f32[6,128,128]{2,1,0:T(8,128)} %get-tuple-element.5) | copy-start | bytes 1179652
where the time goes:
time: 46.1 us; the launch traced here: 46 us
  Pallas kernels  40.7 us (88%)
  local copies, waits for them, and re-layouts  4.66 us (10%)
  between operations  0.65 us (1%)
    pallas_call x1, Pallas kernels, body(): pl.pallas_call(kernel, out_shape=(jax.ShapeDtypeStruct((2 * PLANES, ROWS,...  40.7 us
    unnamed x4, local copies, waits for them, and re-layouts  4.66 us

commit v1 on v0

--- a/solution.py
+++ b/solution.py
@@ -15,6 +15,8 @@
 CAP = 4
 SIGMAS = (1.5, 3.0)
 GROUP = 4
+BATCH = 16
+TURN = 8
 MESH = pl.DeviceIdType.MESH
 BF16, F32 = jnp.bfloat16, jnp.float32
 
@@ -67,13 +69,13 @@
 
 def kernel(
     vel_hbm, ids, used, pos_hbm, bx_hbm, by_hbm, pack_hbm, unpack_hbm,
-    filt_hbm, samp_ref,
+    filt, samp_ref,
     vel, pos, bx, by, pack, unpack,
     rows_first, rows_last, rows_after, rows_before,
     cols_first, cols_last, cols_after, cols_before, corners,
-    halo, filt, table,
+    halo, table, blocks,
     pos_send, pos_recv, out_send, out_recv,
-    in_sems, halo_send, halo_recv, pos_sems, out_sems, filt_sem,
+    in_sems, halo_send, halo_recv, pos_sems, out_sems,
 ):
     ix, iy = lax.axis_index("gx"), lax.axis_index("gy")
     me = ix * GY + iy
@@ -184,18 +186,27 @@
                     got = jnp.dot(wide, by[width], preferred_element_type=F32)
                     filt[width * PLANES + 2 * pair + parity, :, 256 * half : 256 * half + 256] = got.astype(BF16)
                     results.append(got)
-                first_row = pl.multiple_of(width * PLANES * 8 + pair * 16, 16)
                 for block_row in range(ROWS // 8):
                     both = jnp.concatenate(
                         [got[8 * block_row : 8 * block_row + 8] for got in results], axis=0
                     ).astype(BF16)
                     for tile in range(2):
-                        table[block_row * 4 + half * 2 + tile, pl.ds(first_row, 16), :] = both[
+                        table[block_row * 4 + half * 2 + tile, width * (PLANES // 2) + pair] = both[
                             :, 128 * tile : 128 * tile + 128
                         ]
 
-    store = pltpu.make_async_copy(filt, filt_hbm, filt_sem)
-    store.start()
+
+    square = lambda axis: lax.broadcasted_iota(jnp.int32, (128, 128), axis)
+    unit = jnp.where(square(0) == square(1), 1.0, 0.0).astype(BF16)
+
+    @pl.loop(0, 64 // TURN)
+    def _(step):
+        for part in range(TURN):
+            tile = step * TURN + part
+            turned = lax.dot_general(
+                unit, table[tile].reshape(192, 128), (((1,), (1,)), ((), ())), preferred_element_type=F32
+            )
+            blocks[pl.ds(tile * 16, 16)] = turned.reshape(16, 8, 192)
 
     others = pl.ds(0, DEVICES - 1)
     pltpu.make_async_remote_copy(
@@ -204,30 +215,34 @@
     ).wait()
 
     lane_slot = lax.shift_right_logical(lax.broadcasted_iota(jnp.int32, (1, 128), 1), 5)
-    rows128 = lax.broadcasted_iota(jnp.int32, (128, 128), 0).astype(F32)
     rows8 = lax.broadcasted_iota(jnp.int32, (8, 128), 0).astype(F32)
-
-    def sample(owner):
-        numbers = [ids[q, owner] for q in range(CAP)]
-        blocks = jnp.concatenate([table[lax.shift_right_logical(n, 4)] for n in numbers], axis=1)
-        place = [(n & 15) * 8 for n in numbers]
-        offset = jnp.where(
-            lane_slot < 2,
-            jnp.where(lane_slot == 0, place[0], place[1]),
-            jnp.where(lane_slot == 2, place[2], place[3]),
-        ).astype(F32)
-        spot = pos_recv[owner]
-        along_x, along_y, along_z = 7.0 * spot[0:1], 7.0 * spot[1:2], 3.0 * spot[2:3]
-        target = jnp.where(lane_slot < used[0, owner], offset + along_y, -1000.0)
-        weights = jnp.concatenate(
-            [hat(rows128 - jnp.where(lane_slot == q, target, -1000.0)).astype(BF16) for q in range(CAP)], axis=0
+    empty = jnp.zeros((32, 128), BF16)
+
+    def sample(owners):
+        weights = []
+        listed = [blocks[ids[q, owner]] for owner in owners for q in range(CAP)]
+        for u, owner in enumerate(owners):
+            spot = pos_recv[owner]
+            weight_y = jnp.where(lane_slot < used[0, owner], hat(rows8 - 7.0 * spot[1:2]), 0.0)
+            mine = jnp.concatenate(
+                [jnp.where(lane_slot == q, weight_y, 0.0) for q in range(CAP)], axis=0
+            ).astype(BF16)
+            weights.append(jnp.concatenate([mine if v == u else empty for v in range(GROUP)], axis=0))
+        picked = lax.dot_general(
+            jnp.concatenate(listed, axis=0).astype(BF16),
+            jnp.concatenate(weights, axis=1),
+            (((0,), (0,)), ((), ())),
+            preferred_element_type=F32,
         )
-        picked = jnp.dot(blocks, weights, preferred_element_type=F32).reshape(6, 4, 8, 128)
-        weight_x = hat(rows8 - along_x)
-        total = picked[:, 0] * (weight_x * hat(along_z))
-        for z in range(1, 4):
-            total = total + picked[:, z] * (weight_x * hat(along_z - float(z)))
-        out_send[owner] = jnp.sum(total, axis=1)
+        for u, owner in enumerate(owners):
+            spot = pos_recv[owner]
+            along_x, along_z = 7.0 * spot[0:1], 3.0 * spot[2:3]
+            mine = picked[:, 128 * u : 128 * u + 128].reshape(6, 4, 8, 128)
+            weight_x = hat(rows8 - along_x)
+            total = mine[:, 0] * (weight_x * hat(along_z))
+            for z in range(1, 4):
+                total = total + mine[:, z] * (weight_x * hat(along_z - float(z)))
+            out_send[owner] = jnp.sum(total, axis=1)
 
     def reply(owner):
         pltpu.make_async_remote_copy(
@@ -235,22 +250,28 @@
             device_id=device_of(owner), device_id_type=MESH,
         ).start()
 
-    first = [(me + k) & (DEVICES - 1) for k in range(GROUP)]
-    for owner in first:
-        sample(owner)
-    for owner in first[1:]:
+    def batch(number):
+        return [(me + 1 + number * BATCH + k) & (DEVICES - 1) for k in range(BATCH)]
+
+    def sample_batch(owners):
+        for start in range(0, BATCH, GROUP):
+            sample(owners[start : start + GROUP])
+
+    batches = DEVICES // BATCH
+
+    @pl.loop(0, batches - 1)
+    def _(number):
+        owners = batch(number)
+        sample_batch(owners)
+        for owner in owners:
+            reply(owner)
+
+    owners = batch(batches - 1)
+    sample_batch(owners)
+    for owner in owners[:-1]:
         reply(owner)
     out_recv[me] = out_send[me]
 
-    @pl.loop(1, DEVICES // GROUP)
-    def _(group):
-        owners = [(me + group * GROUP + k) & (DEVICES - 1) for k in range(GROUP)]
-        for owner in owners:
-            sample(owner)
-        for owner in owners:
-            reply(owner)
-
-    store.wait()
     for copy in halo_copies:
         copy.wait_send()
     pltpu.make_async_remote_copy(
@@ -264,16 +285,17 @@
 def body(velocity, block_ids, counts, positions):
     tables = [jnp.asarray(t) for t in constant_tables()]
     hbm = pl.BlockSpec(memory_space=pl.ANY)
+    fixed = pl.BlockSpec(memory_space=pltpu.HBM)
     smem = pl.BlockSpec(memory_space=pltpu.SMEM)
     vmem = pl.BlockSpec(memory_space=pltpu.VMEM)
     filtered, sampled = pl.pallas_call(
         kernel,
         out_shape=(
-            jax.ShapeDtypeStruct((2 * PLANES, ROWS, COLS), BF16),
-            jax.ShapeDtypeStruct((6, DEVICES, 128), F32),
+            pltpu.VMEM((2 * PLANES, ROWS, COLS), BF16),
+            pltpu.VMEM((6, DEVICES, 128), F32),
         ),
-        in_specs=[hbm, smem, smem, hbm, hbm, hbm, hbm, hbm],
-        out_specs=(hbm, vmem),
+        in_specs=[fixed, smem, smem, fixed, fixed, fixed, fixed, fixed],
+        out_specs=(vmem, vmem),
         scratch_shapes=[
             pltpu.VMEM((PLANES, ROWS, COLS), BF16),
             pltpu.VMEM((3, DEVICES, 128), F32),
@@ -282,8 +304,8 @@
             *[pltpu.VMEM((ROWS, 128), BF16)] * 4,
             pltpu.VMEM((4, 16, 128), BF16),
             pltpu.VMEM((PLANES, 2 * ROWS, 128), BF16),
-            pltpu.VMEM((2 * PLANES, ROWS, COLS), BF16),
-            pltpu.VMEM((64, 192, 128), BF16),
+            pltpu.VMEM((64, 12, 16, 128), BF16),
+            pltpu.VMEM((1024, 8, 192), F32),
             pltpu.VMEM((DEVICES, 4, 128), F32),
             pltpu.VMEM((DEVICES, 4, 128), F32),
             pltpu.VMEM((DEVICES, 6, 128), F32),
@@ -293,10 +315,9 @@
             pltpu.SemaphoreType.DMA((8,)),
             pltpu.SemaphoreType.DMA((2,)),
             pltpu.SemaphoreType.DMA((2,)),
-            pltpu.SemaphoreType.DMA,
         ],
         compiler_params=pltpu.CompilerParams(
-            collective_id=0, has_side_effects=True, vmem_limit_bytes=63 * 1024 * 1024
+            collective_id=0, has_side_effects=True, vmem_limit_bytes=60 * 1024 * 1024
         ),
         name="filter_and_sample",
     )(

time: 46.1 us -> 38.4 us (0.83)
  the two profiles are of different devices: /device:TPU:0 before, /device:TPU:1 now
where the time goes in v1:
time: 38.4 us; the launch traced here: 38.3 us
  Pallas kernels  35.3 us (92%)
  local copies, waits for them, and re-layouts  2.41 us (6%)
  between operations  0.64 us (2%)
    pallas_call x1, Pallas kernels, body(): pl.pallas_call(kernel, out_shape=(pltpu.VMEM((2 * PLANES, ROWS, COLS), BF...  35.3 us
    unnamed x2, local copies, waits for them, and re-layouts  2.41 us

profile of v1, /device:TPU:1, one launch (start us, length us, event | category | flops | bytes accessed | tf_op | source)
XLA Modules:
  0.0 38.3 jit_solution(5746267952888295991)
XLA Ops:
  0.6 35.3 %filter_and_sample.1 = (bf16[24,128,512]{2,1,0:T(8,128)(2,1)S(1)}, f32[6,128,128]{2,1,0:T(8,128)S(1)}) custom-call(bf16[12,128,512]{2,1,0:T(8,128)(2,1)} %bitcast.12, s32[4,128]{1,0:T(4,128)} %bitcast.14, s32[1,128]{1,0:T(1,128)} %bitcast.15, f32[3,128,128]{2,1,0:T(8,128)} %bitcast.13, bf16[3,256,160]{2,1,0:T(8,128)(2,1)} %constant.8.clone.bx_hbm, ...), custom_call_target="tpu_custom_call" | custom-call | tf_op jit(solution)/shard_map/filter_and_sample/pallas_call | solution.py:291
  35.9 1.7 %copy.13 = bf16[2,3,4,128,512]{4,3,2,1,0:T(8,128)(2,1)} copy(bf16[2,3,4,128,512]{4,3,2,1,0:T(8,128)(2,1)S(1)} %bitcast.10) | data formatting | bytes 6291456
  37.6 0.7 %copy.14 = f32[2,3,1,1,128,128]{5,4,3,2,1,0:T(8,128)} copy(f32[2,3,1,1,128,128]{5,4,3,2,1,0:T(8,128)S(1)} %bitcast.11) | data formatting | bytes 786432

commit v2 on v1

--- a/solution.py
+++ b/solution.py
@@ -16,8 +16,8 @@
 SIGMAS = (1.5, 3.0)
 GROUP = 4
 BATCH = 16
-TURN = 8
-MESH = pl.DeviceIdType.MESH
+TURN = 16
+MESH, LOGICAL = pl.DeviceIdType.MESH, pl.DeviceIdType.LOGICAL
 BF16, F32 = jnp.bfloat16, jnp.float32
 
 
@@ -69,12 +69,12 @@
 
 def kernel(
     vel_hbm, ids, used, pos_hbm, bx_hbm, by_hbm, pack_hbm, unpack_hbm,
-    filt, samp_ref,
+    filt, out_recv,
     vel, pos, bx, by, pack, unpack,
     rows_first, rows_last, rows_after, rows_before,
     cols_first, cols_last, cols_after, cols_before, corners,
-    halo, table, blocks,
-    pos_send, pos_recv, out_send, out_recv,
+    table, blocks,
+    pos_send, pos_recv, out_send,
     in_sems, halo_send, halo_recv, pos_sems, out_sems,
 ):
     ix, iy = lax.axis_index("gx"), lax.axis_index("gy")
@@ -92,11 +92,24 @@
     barrier = pltpu.get_barrier_semaphore()
 
     def device_of(number):
-        return (lax.shift_right_logical(number, 2), number & (GY - 1))
-
-    @pl.loop(1, DEVICES)
-    def _(k):
-        pl.semaphore_signal(barrier, 1, device_id=device_of((me + k) & (DEVICES - 1)), device_id_type=MESH)
+        return number
+
+    def greet(distance):
+        pl.semaphore_signal(
+            barrier, 1, device_id=device_of((me + distance) & (DEVICES - 1)), device_id_type=LOGICAL
+        )
+
+    for near in range(1, 10):
+        greet(near)
+        greet(DEVICES - near)
+
+    @pl.loop(1, 7)
+    def _(step):
+        for near in range(1, 10):
+            greet(step * 9 + near)
+            greet(DEVICES - step * 9 - near)
+
+    greet(DEVICES // 2)
 
     loads[0].wait()
     for c in range(3):
@@ -140,13 +153,20 @@
     for copy in halo_copies:
         copy.start()
 
-    @pl.loop(1, DEVICES)
-    def _(k):
-        other = (me + k) & (DEVICES - 1)
+    def send_place(distance):
+        other = (me + distance) & (DEVICES - 1)
         pltpu.make_async_remote_copy(
             pos_send.at[other], pos_recv.at[me], pos_sems.at[0], pos_sems.at[1],
-            device_id=device_of(other), device_id_type=MESH,
+            device_id=device_of(other), device_id_type=LOGICAL,
         ).start()
+
+    send_place(DEVICES // 2)
+
+    @pl.loop(0, 7)
+    def _(step):
+        for near in range(1, 10):
+            send_place(step * 9 + near)
+            send_place(DEVICES - step * 9 - near)
 
     for load in loads[3:]:
         load.wait()
@@ -160,13 +180,12 @@
         ],
         axis=1,
     )
-    for p in range(PLANES):
-        lanes = pl.ds(128 * p, 128)
-        spread = jnp.dot(packed, unpack[:, lanes], preferred_element_type=F32).astype(BF16)
-        halo[p] = jnp.dot(bx[2], spread, preferred_element_type=F32).astype(BF16)
+    aside = jnp.dot(bx[2], packed, preferred_element_type=F32).astype(BF16)
 
     @pl.loop(0, PLANES // 2)
     def _(pair):
+        lanes = pl.ds(pl.multiple_of(256 * pair, 256), 256)
+        edges = jnp.dot(aside, unpack[:, lanes], preferred_element_type=F32).astype(BF16)
         smooth = []
         for parity in range(2):
             tall = jnp.concatenate([vel[2 * pair + parity], rows_before[pair], rows_after[pair]], axis=0)
@@ -176,7 +195,7 @@
             for half in range(2):
                 results = []
                 for parity in range(2):
-                    edge = halo[2 * pair + parity, part, :]
+                    edge = edges[part, 128 * parity : 128 * parity + 128]
                     inner = smooth[parity][part]
                     wide = (
                         jnp.concatenate([edge, inner[:, :384]], axis=1)
@@ -203,9 +222,12 @@
     def _(step):
         for part in range(TURN):
             tile = step * TURN + part
-            turned = lax.dot_general(
-                unit, table[tile].reshape(192, 128), (((1,), (1,)), ((), ())), preferred_element_type=F32
-            )
+            if True:
+                turned = table[tile].reshape(192, 128).T.astype(F32)
+            else:
+                turned = lax.dot_general(
+                    unit, table[tile].reshape(192, 128), (((1,), (1,)), ((), ())), preferred_element_type=F32
+                )
             blocks[pl.ds(tile * 16, 16)] = turned.reshape(16, 8, 192)
 
     others = pl.ds(0, DEVICES - 1)
@@ -247,7 +269,7 @@
     def reply(owner):
         pltpu.make_async_remote_copy(
             out_send.at[owner], out_recv.at[me], out_sems.at[0], out_sems.at[1],
-            device_id=device_of(owner), device_id_type=MESH,
+            device_id=device_of(owner), device_id_type=LOGICAL,
         ).start()
 
     def batch(number):
@@ -278,8 +300,20 @@
         out_send.at[others], out_recv.at[others], out_sems.at[0], out_sems.at[1],
         device_id=(x_next, iy), device_id_type=MESH,
     ).wait()
+
+
+def finish(filt, got, filt_out, samp_out, landed, samp, sems):
+    first = pltpu.make_async_copy(got, landed, sems.at[0])
+    second = pltpu.make_async_copy(filt, filt_out, sems.at[1])
+    first.start()
+    second.start()
+    first.wait()
     for c in range(6):
-        samp_ref[c] = out_recv[:, c, :]
+        samp[c] = landed[:, c, :]
+    third = pltpu.make_async_copy(samp, samp_out, sems.at[2])
+    third.start()
+    third.wait()
+    second.wait()
 
 
 def body(velocity, block_ids, counts, positions):
@@ -288,11 +322,11 @@
     fixed = pl.BlockSpec(memory_space=pltpu.HBM)
     smem = pl.BlockSpec(memory_space=pltpu.SMEM)
     vmem = pl.BlockSpec(memory_space=pltpu.VMEM)
-    filtered, sampled = pl.pallas_call(
+    filtered, landed = pl.pallas_call(
         kernel,
         out_shape=(
             pltpu.VMEM((2 * PLANES, ROWS, COLS), BF16),
-            pltpu.VMEM((6, DEVICES, 128), F32),
+            pltpu.VMEM((DEVICES, 6, 128), F32),
         ),
         in_specs=[fixed, smem, smem, fixed, fixed, fixed, fixed, fixed],
         out_specs=(vmem, vmem),
@@ -303,12 +337,10 @@
             *[pltpu.VMEM((PLANES // 2, 16, COLS), BF16)] * 4,
             *[pltpu.VMEM((ROWS, 128), BF16)] * 4,
             pltpu.VMEM((4, 16, 128), BF16),
-            pltpu.VMEM((PLANES, 2 * ROWS, 128), BF16),
             pltpu.VMEM((64, 12, 16, 128), BF16),
             pltpu.VMEM((1024, 8, 192), F32),
             pltpu.VMEM((DEVICES, 4, 128), F32),
             pltpu.VMEM((DEVICES, 4, 128), F32),
-            pltpu.VMEM((DEVICES, 6, 128), F32),
             pltpu.VMEM((DEVICES, 6, 128), F32),
             pltpu.SemaphoreType.DMA((6,)),
             pltpu.SemaphoreType.DMA((8,)),
@@ -327,6 +359,22 @@
         positions.reshape(3, DEVICES, 128),
         *tables,
     )
+    filtered, sampled = pl.pallas_call(
+        finish,
+        out_shape=(
+            jax.ShapeDtypeStruct((2 * PLANES, ROWS, COLS), BF16),
+            jax.ShapeDtypeStruct((6, DEVICES, 128), F32),
+        ),
+        in_specs=[hbm, hbm],
+        out_specs=(hbm, hbm),
+        scratch_shapes=[
+            pltpu.VMEM((DEVICES, 6, 128), F32),
+            pltpu.VMEM((6, DEVICES, 128), F32),
+            pltpu.SemaphoreType.DMA((3,)),
+        ],
+        compiler_params=pltpu.CompilerParams(vmem_limit_bytes=2 * 1024 * 1024),
+        name="finish",
+    )(filtered, landed)
     return filtered.reshape(2, 3, 4, ROWS, COLS), sampled.reshape(2, 3, 1, 1, DEVICES, 128)
 
 

time: 38.4 us -> 34.4 us (0.90)
  local copies, waits for them, and re-layouts: 2.41 us -> 0 us
  Pallas kernels: 35.3 us -> 33.6 us
    pallas_call x1, Pallas kernels: 35.3 us -> 31.7 us  [body(): pl.pallas_call(kernel, out_shape=(pltpu.VMEM((2 * PLANES, ROWS, COLS), BF...]
    unnamed x2 -> x0, local copies, waits for them, and re-layouts: 2.41 us -> none
    pallas_call x0 -> x1, Pallas kernels: none -> 1.85 us  [body(): pl.pallas_call(finish, out_shape=(jax.ShapeDtypeStruct((2 * PLANES, ROWS,...]
where the time goes in v2:
time: 34.4 us; the launch traced here: 34.2 us
  Pallas kernels  33.6 us (98%)
  between operations  0.64 us (2%)
    pallas_call x1, Pallas kernels, body(): pl.pallas_call(kernel, out_shape=(pltpu.VMEM((2 * PLANES, ROWS, COLS), BF...  31.7 us
    pallas_call x1, Pallas kernels, body(): pl.pallas_call(finish, out_shape=(jax.ShapeDtypeStruct((2 * PLANES, ROWS,...  1.85 us

profile of v2, /device:TPU:1, one launch (start us, length us, event | category | flops | bytes accessed | tf_op | source)
XLA Modules:
  0.0 34.2 jit_solution(9701854960215869809)
XLA Ops:
  0.6 31.7 %filter_and_sample.1 = (bf16[24,128,512]{2,1,0:T(8,128)(2,1)S(1)}, f32[128,6,128]{2,1,0:T(8,128)S(1)}) custom-call(bf16[12,128,512]{2,1,0:T(8,128)(2,1)} %bitcast.10, s32[4,128]{1,0:T(4,128)} %bitcast.12, s32[1,128]{1,0:T(1,128)} %bitcast.13, f32[3,128,128]{2,1,0:T(8,128)} %bitcast.11, bf16[3,256,160]{2,1,0:T(8,128)(2,1)} %constant.8.clone.bx_hbm, ...), custom_call_target="tpu_custom_call" | custom-call | tf_op jit(solution)/shard_map/filter_and_sample/pallas_call | solution.py:325
  32.4 1.9 %finish.1 = (bf16[24,128,512]{2,1,0:T(8,128)(2,1)}, f32[6,128,128]{2,1,0:T(8,128)}) custom-call(bf16[24,128,512]{2,1,0:T(8,128)(2,1)S(1)} %get-tuple-element.6.filt, f32[128,6,128]{2,1,0:T(8,128)S(1)} %get-tuple-element.7.got), custom_call_target="tpu_custom_call" | custom-call | tf_op jit(solution)/shard_map/finish/pallas_call | solution.py:362

commit v3 on v2

--- a/solution.py
+++ b/solution.py
@@ -73,7 +73,7 @@
     vel, pos, bx, by, pack, unpack,
     rows_first, rows_last, rows_after, rows_before,
     cols_first, cols_last, cols_after, cols_before, corners,
-    table, blocks,
+    early, table, blocks,
     pos_send, pos_recv, out_send,
     in_sems, halo_send, halo_recv, pos_sems, out_sems,
 ):
@@ -170,6 +170,14 @@
 
     for load in loads[3:]:
         load.wait()
+
+    @pl.loop(0, PLANES // 2)
+    def _(pair):
+        for parity in range(2):
+            early[2 * pair + parity] = jnp.dot(
+                bx[2, :, :ROWS], vel[2 * pair + parity], preferred_element_type=F32
+            ).astype(BF16)
+
     for copy in halo_copies:
         copy.wait_recv()
 
@@ -189,14 +197,30 @@
         smooth = []
         for parity in range(2):
             tall = jnp.concatenate([vel[2 * pair + parity], rows_before[pair], rows_after[pair]], axis=0)
-            smooth.append(jnp.dot(bx[parity], tall, preferred_element_type=F32).astype(BF16))
+            ends = jnp.concatenate(
+                [bx[parity, start : start + 16] for start in (0, ROWS - 16, ROWS, 2 * ROWS - 16)], axis=0
+            )
+            late = jnp.dot(ends, tall, preferred_element_type=F32).astype(BF16)
+            smooth.append(
+                [
+                    jnp.concatenate(
+                        [
+                            late[32 * width : 32 * width + 16],
+                            early[2 * pair + parity, width * ROWS + 16 : width * ROWS + ROWS - 16],
+                            late[32 * width + 16 : 32 * width + 32],
+                        ],
+                        axis=0,
+                    )
+                    for width in range(2)
+                ]
+            )
         for width in range(2):
             part = slice(width * ROWS, (width + 1) * ROWS)
             for half in range(2):
                 results = []
                 for parity in range(2):
                     edge = edges[part, 128 * parity : 128 * parity + 128]
-                    inner = smooth[parity][part]
+                    inner = smooth[parity][width]
                     wide = (
                         jnp.concatenate([edge, inner[:, :384]], axis=1)
                         if half == 0
@@ -273,7 +297,12 @@
         ).start()
 
     def batch(number):
-        return [(me + 1 + number * BATCH + k) & (DEVICES - 1) for k in range(BATCH)]
+        steps = [number * BATCH + k for k in range(BATCH)]
+        codes = [
+            (j & 64) | ((j & 4) << 2) | ((j & 16) >> 3) | ((j & 1) << 5) | (j & 8) | ((j & 32) >> 5) | ((j & 2) << 1)
+            for j in steps
+        ]
+        return [me ^ (((j ^ 86) & 86) | ((j ^ (j >> 1)) & 41)) for j in codes]
 
     def sample_batch(owners):
         for start in range(0, BATCH, GROUP):
@@ -337,6 +366,7 @@
             *[pltpu.VMEM((PLANES // 2, 16, COLS), BF16)] * 4,
             *[pltpu.VMEM((ROWS, 128), BF16)] * 4,
             pltpu.VMEM((4, 16, 128), BF16),
+            pltpu.VMEM((PLANES, 2 * ROWS, COLS), BF16),
             pltpu.VMEM((64, 12, 16, 128), BF16),
             pltpu.VMEM((1024, 8, 192), F32),
             pltpu.VMEM((DEVICES, 4, 128), F32),

time: 34.4 us -> 33.7 us (0.980)
  Pallas kernels: 33.6 us -> 32.9 us
    pallas_call x1, Pallas kernels: 31.7 us -> 31.1 us  [body(): pl.pallas_call(kernel, out_shape=(pltpu.VMEM((2 * PLANES, ROWS, COLS), BF...]
where the time goes in v3:
time: 33.7 us; the launch traced here: 33.6 us
  Pallas kernels  32.9 us (98%)
  between operations  0.64 us (2%)
    pallas_call x1, Pallas kernels, body(): pl.pallas_call(kernel, out_shape=(pltpu.VMEM((2 * PLANES, ROWS, COLS), BF...  31.1 us
    pallas_call x1, Pallas kernels, body(): pl.pallas_call(finish, out_shape=(jax.ShapeDtypeStruct((2 * PLANES, ROWS,...  1.85 us

profile of v3, /device:TPU:1, one launch (start us, length us, event | category | flops | bytes accessed | tf_op | source)
XLA Modules:
  0.0 33.6 jit_solution(2620452651666028499)
XLA Ops:
  0.6 31.1 %filter_and_sample.1 = (bf16[24,128,512]{2,1,0:T(8,128)(2,1)S(1)}, f32[128,6,128]{2,1,0:T(8,128)S(1)}) custom-call(bf16[12,128,512]{2,1,0:T(8,128)(2,1)} %bitcast.10, s32[4,128]{1,0:T(4,128)} %bitcast.12, s32[1,128]{1,0:T(1,128)} %bitcast.13, f32[3,128,128]{2,1,0:T(8,128)} %bitcast.11, bf16[3,256,160]{2,1,0:T(8,128)(2,1)} %constant.8.clone.bx_hbm, ...), custom_call_target="tpu_custom_call" | custom-call | tf_op jit(solution)/shard_map/filter_and_sample/pallas_call | solution.py:354
  31.7 1.9 %finish.1 = (bf16[24,128,512]{2,1,0:T(8,128)(2,1)}, f32[6,128,128]{2,1,0:T(8,128)}) custom-call(bf16[24,128,512]{2,1,0:T(8,128)(2,1)S(1)} %get-tuple-element.6.filt, f32[128,6,128]{2,1,0:T(8,128)S(1)} %get-tuple-element.7.got), custom_call_target="tpu_custom_call" | custom-call | tf_op jit(solution)/shard_map/finish/pallas_call | solution.py:392

commit v4 on v3

--- a/solution.py
+++ b/solution.py
@@ -15,7 +15,7 @@
 CAP = 4
 SIGMAS = (1.5, 3.0)
 GROUP = 4
-BATCH = 16
+BATCH = 32
 TURN = 16
 MESH, LOGICAL = pl.DeviceIdType.MESH, pl.DeviceIdType.LOGICAL
 BF16, F32 = jnp.bfloat16, jnp.float32
@@ -54,13 +54,14 @@
     along_x = np.stack(tables)
     k, n = np.arange(512)[:, None], np.arange(256)[None, :]
     along_y = tap_lookup(taps, k - 128 - n + REACH)
+    edge_y = np.concatenate([along_y[:, :128, :128] + along_y[:, 256:384, :128], along_y[:, 128:256, :128]], axis=1)
     plane, lane = np.arange(PLANES * 128)[:, None] // 128, np.arange(PLANES * 128)[:, None] % 128
     n = np.arange(128)[None, :]
     last = (lane >= 120) & (n == 8 * plane + lane - 120)
     first = (lane < 8) & (n == 8 * plane + lane)
     pack = np.stack([first, last]).astype(np.float32)
     unpack = np.concatenate([last.T, first.T], axis=0).astype(np.float32)
-    return [np.asarray(t, np.float32).astype(ml_dtypes.bfloat16) for t in (along_x, along_y, pack, unpack)]
+    return [np.asarray(t, np.float32).astype(ml_dtypes.bfloat16) for t in (along_x, along_y, pack, unpack, edge_y)]
 
 
 def hat(distance):
@@ -68,9 +69,9 @@
 
 
 def kernel(
-    vel_hbm, ids, used, pos_hbm, bx_hbm, by_hbm, pack_hbm, unpack_hbm,
+    vel_hbm, ids, used, pos_hbm, bx_hbm, by_hbm, pack_hbm, unpack_hbm, be_hbm,
     filt, out_recv,
-    vel, pos, bx, by, pack, unpack,
+    vel, pos, bx, by, pack, unpack, be,
     rows_first, rows_last, rows_after, rows_before,
     cols_first, cols_last, cols_after, cols_before, corners,
     early, table, blocks,
@@ -83,7 +84,7 @@
     loads = [
         pltpu.make_async_copy(src, dst, in_sems.at[i])
         for i, (src, dst) in enumerate(
-            ((pos_hbm, pos), (vel_hbm, vel), (pack_hbm, pack), (unpack_hbm, unpack), (bx_hbm, bx), (by_hbm, by))
+            ((pos_hbm, pos), (vel_hbm, vel), (pack_hbm, pack), (unpack_hbm, unpack), (bx_hbm, bx), (by_hbm, by), (be_hbm, be))
         )
     ]
     for load in loads:
@@ -171,12 +172,33 @@
     for load in loads[3:]:
         load.wait()
 
+    def put(width, pair, results, first_row, first_column):
+        for parity, got in enumerate(results):
+            filt[
+                width * PLANES + 2 * pair + parity,
+                first_row : first_row + got.shape[0],
+                first_column : first_column + got.shape[1],
+            ] = got.astype(BF16)
+        for block_row in range(results[0].shape[0] // 8):
+            both = jnp.concatenate([got[8 * block_row : 8 * block_row + 8] for got in results], axis=0).astype(BF16)
+            for tile in range(results[0].shape[1] // 128):
+                table[
+                    (first_row // 8 + block_row) * 4 + first_column // 128 + tile, width * (PLANES // 2) + pair
+                ] = both[:, 128 * tile : 128 * tile + 128]
+
     @pl.loop(0, PLANES // 2)
     def _(pair):
+        whole = []
         for parity in range(2):
-            early[2 * pair + parity] = jnp.dot(
-                bx[2, :, :ROWS], vel[2 * pair + parity], preferred_element_type=F32
-            ).astype(BF16)
+            whole.append(
+                jnp.dot(bx[2, :, :ROWS], vel[2 * pair + parity], preferred_element_type=F32).astype(BF16)
+            )
+            early[2 * pair + parity] = whole[parity]
+        for width in range(2):
+            results = [
+                jnp.dot(w[width * ROWS : (width + 1) * ROWS], by[width], preferred_element_type=F32) for w in whole
+            ]
+            put(width, pair, results, 0, 128)
 
     for copy in halo_copies:
         copy.wait_recv()
@@ -188,19 +210,21 @@
         ],
         axis=1,
     )
+    lane_of = lax.broadcasted_iota(jnp.int32, (128, 128), 1).astype(BF16)
     aside = jnp.dot(bx[2], packed, preferred_element_type=F32).astype(BF16)
 
     @pl.loop(0, PLANES // 2)
     def _(pair):
         lanes = pl.ds(pl.multiple_of(256 * pair, 256), 256)
         edges = jnp.dot(aside, unpack[:, lanes], preferred_element_type=F32).astype(BF16)
-        smooth = []
+        smooth, tips = [], []
         for parity in range(2):
             tall = jnp.concatenate([vel[2 * pair + parity], rows_before[pair], rows_after[pair]], axis=0)
             ends = jnp.concatenate(
                 [bx[parity, start : start + 16] for start in (0, ROWS - 16, ROWS, 2 * ROWS - 16)], axis=0
             )
             late = jnp.dot(ends, tall, preferred_element_type=F32).astype(BF16)
+            tips.append(late)
             smooth.append(
                 [
                     jnp.concatenate(
@@ -216,28 +240,23 @@
             )
         for width in range(2):
             part = slice(width * ROWS, (width + 1) * ROWS)
-            for half in range(2):
+            middle = [
+                jnp.dot(late[32 * width : 32 * width + 32], by[width], preferred_element_type=F32) for late in tips
+            ]
+            put(width, pair, [got[:16] for got in middle], 0, 128)
+            put(width, pair, [got[16:] for got in middle], ROWS - 16, 128)
+            for side in range(2):
                 results = []
                 for parity in range(2):
                     edge = edges[part, 128 * parity : 128 * parity + 128]
                     inner = smooth[parity][width]
-                    wide = (
-                        jnp.concatenate([edge, inner[:, :384]], axis=1)
-                        if half == 0
-                        else jnp.concatenate([inner[:, 128:], edge], axis=1)
-                    )
-                    got = jnp.dot(wide, by[width], preferred_element_type=F32)
-                    filt[width * PLANES + 2 * pair + parity, :, 256 * half : 256 * half + 256] = got.astype(BF16)
-                    results.append(got)
-                for block_row in range(ROWS // 8):
-                    both = jnp.concatenate(
-                        [got[8 * block_row : 8 * block_row + 8] for got in results], axis=0
-                    ).astype(BF16)
-                    for tile in range(2):
-                        table[block_row * 4 + half * 2 + tile, width * (PLANES // 2) + pair] = both[
-                            :, 128 * tile : 128 * tile + 128
-                        ]
-
+                    if side == 0:
+                        beside, own = jnp.where(lane_of < 8.0, inner[:, 128:256], edge), inner[:, :128]
+                    else:
+                        beside, own = jnp.where(lane_of >= 120.0, inner[:, 256:384], edge), inner[:, 384:]
+                    wide = jnp.concatenate([beside, own], axis=1)
+                    results.append(jnp.dot(wide, be[width], preferred_element_type=F32))
+                put(width, pair, results, 0, 384 * side)
 
     square = lambda axis: lax.broadcasted_iota(jnp.int32, (128, 128), axis)
     unit = jnp.where(square(0) == square(1), 1.0, 0.0).astype(BF16)
@@ -357,7 +376,7 @@
             pltpu.VMEM((2 * PLANES, ROWS, COLS), BF16),
             pltpu.VMEM((DEVICES, 6, 128), F32),
         ),
-        in_specs=[fixed, smem, smem, fixed, fixed, fixed, fixed, fixed],
+        in_specs=[fixed, smem, smem, fixed, fixed, fixed, fixed, fixed, fixed],
         out_specs=(vmem, vmem),
         scratch_shapes=[
             pltpu.VMEM((PLANES, ROWS, COLS), BF16),
@@ -372,7 +391,7 @@
             pltpu.VMEM((DEVICES, 4, 128), F32),
             pltpu.VMEM((DEVICES, 4, 128), F32),
             pltpu.VMEM((DEVICES, 6, 128), F32),
-            pltpu.SemaphoreType.DMA((6,)),
+            pltpu.SemaphoreType.DMA((7,)),
             pltpu.SemaphoreType.DMA((8,)),
             pltpu.SemaphoreType.DMA((8,)),
             pltpu.SemaphoreType.DMA((2,)),

time: 33.7 us -> 33.4 us (level)
  no operation moved by 1% of the time
where the time goes in v4:
time: 33.4 us; the launch traced here: 33.3 us
  Pallas kernels  32.7 us (98%)
  between operations  0.64 us (2%)
    pallas_call x1, Pallas kernels, body(): pl.pallas_call(kernel, out_shape=(pltpu.VMEM((2 * PLANES, ROWS, COLS), BF...  30.8 us
    pallas_call x1, Pallas kernels, body(): pl.pallas_call(finish, out_shape=(jax.ShapeDtypeStruct((2 * PLANES, ROWS,...  1.85 us

profile of v4, /device:TPU:1, one launch (start us, length us, event | category | flops | bytes accessed | tf_op | source)
XLA Modules:
  0.0 33.3 jit_solution(10937216307789926809)
XLA Ops:
  0.6 30.8 %filter_and_sample.1 = (bf16[24,128,512]{2,1,0:T(8,128)(2,1)S(1)}, f32[128,6,128]{2,1,0:T(8,128)S(1)}) custom-call(bf16[12,128,512]{2,1,0:T(8,128)(2,1)} %bitcast.10, s32[4,128]{1,0:T(4,128)} %bitcast.12, s32[1,128]{1,0:T(1,128)} %bitcast.13, f32[3,128,128]{2,1,0:T(8,128)} %bitcast.11, bf16[3,256,160]{2,1,0:T(8,128)(2,1)} %constant.10.clone.bx_hbm, ...), custom_call_target="tpu_custom_call" | custom-call | tf_op jit(solution)/shard_map/filter_and_sample/pallas_call | solution.py:373
  31.5 1.9 %finish.1 = (bf16[24,128,512]{2,1,0:T(8,128)(2,1)}, f32[6,128,128]{2,1,0:T(8,128)}) custom-call(bf16[24,128,512]{2,1,0:T(8,128)(2,1)S(1)} %get-tuple-element.6.filt, f32[128,6,128]{2,1,0:T(8,128)S(1)} %get-tuple-element.7.got), custom_call_target="tpu_custom_call" | custom-call | tf_op jit(solution)/shard_map/finish/pallas_call | solution.py:411
